TPU v7x, 256 devices: a whole 4x4x8 slice. The times are simulated.
256 devices in a mesh: dp: 4 (over x), chan: 2 (over z_hi), seq: 32 (over y, z_lo, core).
Axes of the slice: x: 4, y: 4, z: 8 (z_hi: 2, z_lo: 4; z = z_hi * 4 + z_lo), core: 2. Of those that a mesh axis runs over, the one named last changes fastest.
Arguments:
- inputs: bfloat16 [4, 65536, 768], P('dp', 'seq', 'chan'), may hold values from -6 to 6
- gate: bfloat16 [4, 65536, 768], P('dp', 'seq', 'chan'), may hold values from -6 to 6
- cotangent: bfloat16 [4, 65536, 768], P('dp', 'seq', 'chan'), may hold values from -6 to 6
- first_factor: bfloat16 [256, 256, 256], P('seq'), may hold values from -0.375 to 0.375
- second_factor: bfloat16 [256, 256, 256], P('seq'), may hold values from -0.375 to 0.375
Outputs:
- mixed: bfloat16 [4, 65536, 768], P('dp', 'seq', 'chan')
- grad_inputs: bfloat16 [4, 65536, 768], P('dp', 'seq', 'chan')
- grad_first: float32 [256, 256, 256], P('seq', ('dp', 'chan'))
- grad_second: float32 [256, 256, 256], P('seq', ('dp', 'chan'))
All inputs are finite; a program needn't handle non-finite values.
Results may differ from a plain program's by a relative error of at most 0.0057.
Values may be sent and summed in bfloat16 or wider, within the bound.
A program may use at most 64 MiB of HBM per device.

v0:
```python
import jax
import jax.numpy as jnp
from jax import lax
from jax.sharding import PartitionSpec as P


def on_device(inputs, gate, cotangent, first_factor, second_factor):
    seqs_here = inputs.shape[0]
    blocks_here = first_factor.shape[0]
    block = first_factor.shape[1]
    channels = inputs.shape[2]
    shape_four = (seqs_here, blocks_here, block, channels)
    x_blocks = inputs.reshape(shape_four)
    gate_blocks = gate.reshape(shape_four)
    first_mixed = jnp.einsum(
        "ikj,sijc->sikc", first_factor, x_blocks, preferred_element_type=jnp.float32
    ).astype(jnp.bfloat16)
    grad_mixed = (
        cotangent.reshape(shape_four).astype(jnp.float32) * gate_blocks.astype(jnp.float32)
    ).astype(jnp.bfloat16)
    grad_first_t = jnp.einsum(
        "kmi,skmc->skic", second_factor, grad_mixed, preferred_element_type=jnp.float32
    ).astype(jnp.bfloat16)
    piece = lax.all_to_all(first_mixed, "seq", split_axis=2, concat_axis=1, tiled=True)
    second_mixed = jnp.einsum(
        "kmi,sikc->skmc", second_factor, piece, preferred_element_type=jnp.float32
    )
    backward_piece = lax.all_to_all(grad_first_t, "seq", split_axis=2, concat_axis=1, tiled=True)
    grad_x = jnp.einsum(
        "ikj,skic->sijc", first_factor, backward_piece, preferred_element_type=jnp.float32
    )
    mixed = (second_mixed * gate_blocks.astype(jnp.float32)).astype(jnp.bfloat16)
    grad_second_part = jnp.einsum(
        "skmc,sikc->kmi", grad_mixed, piece, preferred_element_type=jnp.float32
    )
    grad_first_part = jnp.einsum(
        "skic,sijc->ikj", backward_piece, x_blocks, preferred_element_type=jnp.float32
    )
    grad_first, grad_second = (
        lax.psum_scatter(grad_first_part, ("dp", "chan"), scatter_dimension=1, tiled=True),
        lax.psum_scatter(grad_second_part, ("dp", "chan"), scatter_dimension=1, tiled=True),
    )
    rows = inputs.shape[1]
    return (
        mixed.reshape(seqs_here, rows, channels),
        grad_x.astype(jnp.bfloat16).reshape(seqs_here, rows, channels),
        grad_first,
        grad_second,
    )


def solution(mesh):
    in_specs = (
        P("dp", "seq", "chan"),
        P("dp", "seq", "chan"),
        P("dp", "seq", "chan"),
        P("seq", None, None),
        P("seq", None, None),
    )
    out_specs = (
        P("dp", "seq", "chan"),
        P("dp", "seq", "chan"),
        P("seq", ("dp", "chan"), None),
        P("seq", ("dp", "chan"), None),
    )
    return jax.shard_map(
        on_device, mesh=mesh, in_specs=in_specs, out_specs=out_specs, check_vma=False
    )
```

profile of v0, /device:TPU:1, one launch (start us, length us, event | category | flops | bytes accessed | tf_op | source)
XLA Modules:
  0.0 270.1 jit_solution(14271135420160050394)
XLA Ops:
  7.2 0.0 copy-start
  7.2 1.4 copy-done
  8.6 1.9 fusion.7
  10.5 2.1 copy.22
  12.5 10.4 %all-to-all-start = ((bf16[1,8,256,384]{3,1,0,2:T(8,128)(2,1)}), bf16[1,8,256,384]{3,1,0,2:T(8,128)(2,1)}, u32[]{:S(2)}, u32[]{:S(2)}) async-start(bf16[1,8,256,384]{3,1,0,2:T(8,128)(2,1)} %copy.22), calls=%async_computation | async-start | bytes 3145728 | tf_op jit(solution)/shard_map/all_to_all | solution.py:24
  22.9 0.0 reduce-scatter.5.cloned.1.call-start
  23.0 3.0 %multiply_convert_fusion = bf16[1,2048,384]{2,1,0:T(8,128)(2,1)} fusion(bf16[1,2048,384]{2,1,0:T(8,128)(2,1)} %param.7, bf16[1,2048,384]{2,1,0:T(8,128)(2,1)S(1)} %copy-done.3), kind=kLoop, calls=%fused_computation.2 | loop fusion | flops 3145728 | bytes 4718592 | tf_op jit(solution)/shard_map/convert_element_type | solution.py:20
  25.9 35.9 %all-to-all-done = bf16[1,8,256,384]{3,1,0,2:T(8,128)(2,1)} async-done(((bf16[1,8,256,384]{3,1,0,2:T(8,128)(2,1)}), bf16[1,8,256,384]{3,1,0,2:T(8,128)(2,1)}, u32[]{:S(2)}, u32[]{:S(2)}) %all-to-all-start) | async-done | bytes 1572896 | tf_op jit(solution)/shard_map/all_to_all | solution.py:24
  61.8 1.7 copy.52
  63.6 0.1 copy-done.2
  63.7 2.6 fusion.4
  66.3 0.0 reduce-scatter.5.cloned.1.call-update
  66.3 0.0 reduce-scatter.3.cloned.1.call-start
  66.4 3.5 %fusion.8 = bf16[1,8,256,384]{2,3,1,0:T(8,128)(2,1)} fusion(bf16[8,256,384]{2,1,0:T(8,128)(2,1)} %bitcast.58, bf16[8,256,256]{2,1,0:T(8,128)(2,1)} %param.9), kind=kOutput, calls=%fused_computation.15 | convolution fusion | flops 403439616 | bytes 4194304 | tf_op jit(solution)/shard_map/kmi,skmc->skic/dot_general | solution.py:21
  69.9 2.9 %copy.26 = bf16[1,8,256,384]{3,1,0,2:T(8,128)(2,1)} copy(bf16[1,8,256,384]{2,3,1,0:T(8,128)(2,1)} %fusion.8) | data formatting | bytes 3145728 | tf_op jit(solution)/shard_map/convert_element_type | solution.py:23
  72.8 66.0 %all_to_all.30 = bf16[1,8,256,384]{3,1,0,2:T(8,128)(2,1)S(1)} all-to-all(bf16[1,8,256,384]{3,1,0,2:T(8,128)(2,1)} %copy.26), channel_id=1, replica_groups=mesh['dp'=4,'chan'=2,'seq'=32] {'seq'}, dimensions={2} | all-to-all | bytes 3145728 | tf_op jit(solution)/shard_map/all_to_all | solution.py:28
  138.8 0.2 copy.51
  139.0 1.1 copy-done.1
  140.1 2.5 fusion.1
  142.7 0.0 reduce-scatter.3.cloned.1.call-update
  142.7 5.1 %convolution_convert_fusion = bf16[8,384,256]{1,2,0:T(8,128)(2,1)} fusion(bf16[8,256,256]{2,1,0:T(8,128)(2,1)} %param.8, bf16[1,32,8,8,384]{4,3,1,2,0:T(8,128)(2,1)} %bitcast.57), kind=kOutput, calls=%fused_computation.3 | convolution fusion | flops 403439616 | bytes 4194304 | tf_op jit(solution)/shard_map/ikj,skic->sijc/dot_general | solution.py:29
  147.8 3.4 %fusion = bf16[1,8,256,384]{3,2,1,0:T(8,128)(2,1)} fusion(bf16[8,256,256]{2,1,0:T(8,128)(2,1)S(1)} %copy-done.5, bf16[1,32,8,8,384]{4,3,1,2,0:T(8,128)(2,1)S(1)} %bitcast.55, bf16[1,8,256,384]{3,2,1,0:T(8,128)(2,1)S(1)} %bitcast.60), kind=kOutput, calls=%fused_computation.1 | convolution fusion | flops 405012480 | bytes 5767168 | tf_op jit(solution)/shard_map/kmi,sikc->skmc/dot_general | solution.py:25
  151.2 15.9 %reduce-scatter.5.cloned.1.call-done = f32[8,32,256]{2,1,0:T(8,128)} async-done(((f32[8,256,256]{2,1,0:T(8,128)}), f32[8,32,256]{2,1,0:T(8,128)}) %reduce-scatter.5.cloned.1.call-update) | async-done | bytes 262160 | tf_op jit(solution)/shard_map/reduce_scatter | solution.py:41
  167.1 96.1 %reduce-scatter.3.cloned.1.call-done = f32[8,32,256]{2,1,0:T(8,128)} async-done(((f32[8,256,256]{2,1,0:T(8,128)}), f32[8,32,256]{2,1,0:T(8,128)}) %reduce-scatter.3.cloned.1.call-update) | async-done | bytes 262160 | tf_op jit(solution)/shard_map/reduce_scatter | solution.py:40
  (8 shorter events, 0.0 us)
Async XLA Ops:
  7.2 1.4 copy-start
  12.5 10.4 %copy-start.3 = (bf16[1,2048,384]{2,1,0:T(8,128)(2,1)S(1)}, bf16[1,2048,384]{2,1,0:T(8,128)(2,1)}, u32[]{:S(2)}) copy-start(bf16[1,2048,384]{2,1,0:T(8,128)(2,1)} %param.6) | copy-start | bytes 4718596
  12.5 49.3 %all-to-all-start = ((bf16[1,8,256,384]{3,1,0,2:T(8,128)(2,1)}), bf16[1,8,256,384]{3,1,0,2:T(8,128)(2,1)}, u32[]{:S(2)}, u32[]{:S(2)}) async-start(bf16[1,8,256,384]{3,1,0,2:T(8,128)(2,1)} %copy.22), calls=%async_computation | async-start | bytes 3145728 | tf_op jit(solution)/shard_map/all_to_all | solution.py:24
  22.9 144.2 %reduce-scatter.5.cloned.1.call-start = ((), (), s32[]{:S(2)}) async-start(), calls=%async_computation.5 | async-start | bytes 2359296 | tf_op jit(solution)/shard_map/reduce_scatter | solution.py:41
  61.8 1.9 copy-start.2
  66.3 196.9 %reduce-scatter.3.cloned.1.call-start = ((), (), s32[]{:S(2)}) async-start(), calls=%async_computation.4 | async-start | bytes 2359296 | tf_op jit(solution)/shard_map/reduce_scatter | solution.py:40
  139.0 1.1 copy-start.1
  142.7 5.1 %copy-start.4 = (bf16[1,2048,384]{2,1,0:T(8,128)(2,1)S(1)}, bf16[1,2048,384]{2,1,0:T(8,128)(2,1)}, u32[]{:S(2)}) copy-start(bf16[1,2048,384]{2,1,0:T(8,128)(2,1)} %param.6) | copy-start | bytes 4718596
  142.7 5.1 %copy-start.5 = (bf16[8,256,256]{2,1,0:T(8,128)(2,1)S(1)}, bf16[8,256,256]{2,1,0:T(8,128)(2,1)}, u32[]{:S(2)}) copy-start(bf16[8,256,256]{2,1,0:T(8,128)(2,1)} %param.9) | copy-start | bytes 3145732
Sparse Core Ops, SparseCore 0:
  66.4 100.6 reduce-scatter.4
  172.3 90.9 reduce-scatter.2
where the time goes:
time: 271 us; the launch traced here: 270 us
  waiting for transfers between devices  148 us (55%)
  blocking collectives  66 us (24%)
  matrix products  19 us (7%)
  between operations  14.1 us (5%)
  starting transfers between devices  10.5 us (4%)
  local copies, waits for them, and re-layouts  9.6 us (4%)
  other arithmetic  2.95 us (1%)
    reduce_scatter x1, waiting for transfers between devices, on_device(): lax.psum_scatter(grad_first_part, ('dp', 'chan'), scatter_dimension=1, ti...  96.1 us
    all_to_all x1, blocking collectives, on_device(): lax.all_to_all(grad_first_t, 'seq', split_axis=2, concat_axis=1, tiled=True)  66 us
    all_to_all x1, waiting for transfers between devices, on_device(): lax.all_to_all(first_mixed, 'seq', split_axis=2, concat_axis=1, tiled=True)  35.9 us
    reduce_scatter x1, waiting for transfers between devices, on_device(): lax.psum_scatter(grad_second_part, ('dp', 'chan'), scatter_dimension=1, t...  15.9 us
    all_to_all x1, starting transfers between devices, on_device(): lax.all_to_all(first_mixed, 'seq', split_axis=2, concat_axis=1, tiled=True)  10.4 us
  transfers between devices with their start and end apart: 3, of which 3 were waited for; matrix products, arithmetic and copies ran while one was open for 8% of the time, Pallas kernels for 0%

commit v1 on v0

v1 whole, which is shorter than its diff:
```python
import jax
import jax.numpy as jnp
from jax import lax
from jax.experimental import pallas as pl
from jax.experimental.pallas import tpu as pltpu
from jax.sharding import PartitionSpec as P

MESH = pl.DeviceIdType.MESH
F32 = jnp.float32
BF16 = jnp.bfloat16

N = 32
B = 8
K = 256
C = 384
W = C // 128
DP = 4
FCH = 2
FR = 64 // FCH
GCH = 4


def dot(a, b, dims):
    return lax.dot_general(a, b, (dims, ((), ())), preferred_element_type=F32)


def kernel(
    x_h, g_h, t_h, ff_h, sf_h,
    mixed_h, gx_h, gf_h, gs_h,
    x_v, g_v, t_v, ff_v, sf_v, tmp, fs, fr, bs, br, mixed_v, gx_v,
    part2, part1, rs2, rr2, rs1, rr1, cs2, cr2, cs1, cr1, out2, out1,
    in_sem, f_send, f_recv, b_send, b_recv, r_send, r_recv, c_send, c_recv, o_sem,
):
    dp = lax.axis_index("dp")
    ch = lax.axis_index("chan")
    me = lax.axis_index("seq")

    loads = {}
    for i in range(B):
        for n, (h, v) in enumerate(((ff_h, ff_v), (x_h, x_v))):
            loads[n, i] = pltpu.make_async_copy(h.at[i], v.at[i], in_sem.at[n, i])
            loads[n, i].start()
    for i in range(B):
        for n, (h, v) in enumerate(((t_h, t_v), (g_h, g_v), (sf_h, sf_v))):
            loads[n + 2, i] = pltpu.make_async_copy(h.at[i], v.at[i], in_sem.at[n + 2, i])
            loads[n + 2, i].start()

    barrier = pltpu.get_barrier_semaphore()

    def greet(s, carry):
        pl.semaphore_signal(
            barrier, inc=1, device_id={"seq": lax.rem(me + s, N)}, device_id_type=MESH
        )
        return carry

    lax.fori_loop(1, N, greet, 0)
    for s in range(1, DP):
        pl.semaphore_signal(
            barrier, inc=1, device_id={"dp": lax.rem(dp + s, DP)}, device_id_type=MESH
        )
    pl.semaphore_signal(barrier, inc=1, device_id={"chan": 1 - ch}, device_id_type=MESH)

    def exchange(src, dst, c, send_sem, recv_sem):
        def one(s, carry):
            to = lax.rem(me + s, N)
            pltpu.make_async_remote_copy(
                src_ref=src.at[c, to],
                dst_ref=dst.at[c, me],
                send_sem=send_sem.at[c],
                recv_sem=recv_sem.at[c],
                device_id={"seq": to},
                device_id_type=MESH,
            ).start()
            return carry

        lax.fori_loop(1, N, one, 0)
        pltpu.make_async_copy(src.at[c, me], dst.at[c, me], recv_sem.at[c]).start()

    def arrived(dst, sem):
        pltpu.make_async_copy(dst, dst, sem).wait()

    for c in range(FCH):
        for p in range(FR // 16):
            both = []
            for i in (c * (B // FCH) + 2 * p, c * (B // FCH) + 2 * p + 1):
                loads[0, i].wait()
                loads[1, i].wait()
                both.append(dot(ff_v[i], x_v[i], ((1,), (0,))).reshape(N, B, C))
            fs[c, :, 16 * p : 16 * p + 16, :] = jnp.concatenate(both, axis=1).astype(BF16)
        if c == 0:
            pl.semaphore_wait(barrier, N - 1 + DP - 1 + 1)
        exchange(fs, fr, c, f_send, f_recv)

    for k in range(B):
        for n in (2, 3, 4):
            loads[n, k].wait()
        t_v[k] = (t_v[k].astype(F32) * g_v[k].astype(F32)).astype(BF16)
        grad = dot(sf_v[k], t_v[k], ((0,), (0,)))
        for w in range(W):
            tmp[w, pl.ds(k, K, stride=B), :] = grad[:, 128 * w : 128 * w + 128]
    for c in range(GCH):

        def pack(q, carry):
            rows = pl.multiple_of(q * 64 + c * 16, 16)
            for w in range(W):
                bs[c, q, :, 128 * w : 128 * w + 128] = tmp[w, pl.ds(rows, 16), :].astype(BF16)
            return carry

        lax.fori_loop(0, N, pack, 0)
        exchange(bs, br, c, b_send, b_recv)

    def reduce_send(src, dst, n):
        for s in range(1, DP):
            to = lax.rem(dp + s, DP)
            pltpu.make_async_remote_copy(
                src_ref=src.at[to],
                dst_ref=dst.at[s - 1],
                send_sem=r_send.at[n],
                recv_sem=r_recv.at[n],
                device_id={"dp": to},
                device_id_type=MESH,
            ).start()

    def summed(part, recv, half, first, count):
        own = pl.multiple_of(dp * 64 + half * 32, 32)
        rows = pl.multiple_of(half * 32, 32)
        total = part[first : first + count, pl.ds(own, 32), :]
        for s in range(DP - 1):
            total = total + recv[s, :, pl.ds(rows, 32), :].astype(F32)
        return total

    def chan_send(part, recv, send, land, out, n, first, count):
        arrived(recv, r_recv.at[n])
        send[...] = summed(part, recv, 1 - ch, first, count).astype(BF16)
        pltpu.make_async_remote_copy(
            src_ref=send,
            dst_ref=land,
            send_sem=c_send.at[n],
            recv_sem=c_recv.at[n],
            device_id={"chan": 1 - ch},
            device_id_type=MESH,
        ).start()
        out[first : first + count] = summed(part, recv, ch, first, count)

    def chan_done(land, out, n, first, count):
        arrived(land, c_recv.at[n])
        out[first : first + count] = out[first : first + count] + land[...].astype(F32)

    for c in range(FCH):
        arrived(fr.at[c], f_recv.at[c])

        def unpack(q, carry):
            rows = pl.multiple_of(q * 64 + c * FR, FR)
            for w in range(W):
                tmp[w, pl.ds(rows, FR), :] = fr[c, q, :, 128 * w : 128 * w + 128].astype(F32)
            return carry

        lax.fori_loop(0, N, unpack, 0)
    stores = []
    for k in range(B):
        piece = jnp.concatenate(
            [tmp[w, pl.ds(k, K, stride=B), :].astype(BF16) for w in range(W)], axis=1
        )
        mixed_v[k] = (dot(sf_v[k], piece, ((1,), (0,))) * g_v[k].astype(F32)).astype(BF16)
        stores.append(pltpu.make_async_copy(mixed_v.at[k], mixed_h.at[k], o_sem.at[0, k]))
        stores[-1].start()
        grad = dot(t_v[k], piece, ((1,), (1,)))
        part2[k] = grad
        for d in range(DP):
            rs2[d, k] = grad[64 * d : 64 * d + 64].astype(BF16)
    reduce_send(rs2, rr2, GCH)

    for c in range(GCH):
        arrived(br.at[c], b_recv.at[c])
        chunk = br[c].astype(F32)
        for h in range(2):
            i = 2 * c + h
            piece = chunk[:, B * h : B * h + B, :].reshape(K, C).astype(BF16)
            grad = dot(piece, x_v[i], ((1,), (1,)))
            part1[i] = grad
            for d in range(DP):
                rs1[c, d, h] = grad[64 * d : 64 * d + 64].astype(BF16)
        reduce_send(rs1.at[c], rr1.at[c], c)
        for h in range(2):
            i = 2 * c + h
            piece = chunk[:, B * h : B * h + B, :].reshape(K, C).astype(BF16)
            gx_v[i] = dot(ff_v[i], piece, ((0,), (0,))).astype(BF16)
            stores.append(pltpu.make_async_copy(gx_v.at[i], gx_h.at[i], o_sem.at[1, i]))
            stores[-1].start()
        if c == 0:
            chan_send(part2, rr2, cs2, cr2, out2, GCH, 0, B)
        else:
            chan_send(part1, rr1.at[c - 1], cs1.at[c - 1], cr1.at[c - 1], out1, c - 1, 2 * c - 2, 2)
    c = GCH - 1
    chan_done(cr2, out2, GCH, 0, B)
    stores.append(pltpu.make_async_copy(out2, gs_h, o_sem.at[2, 0]))
    stores[-1].start()
    chan_send(part1, rr1.at[c], cs1.at[c], cr1.at[c], out1, c, 2 * c, 2)
    for c in range(GCH):
        chan_done(cr1.at[c], out1, c, 2 * c, 2)
    stores.append(pltpu.make_async_copy(out1, gf_h, o_sem.at[2, 1]))
    stores[-1].start()

    for c in range(FCH):
        sent = fs.at[c, pl.ds(0, N - 1)]
        pltpu.make_async_copy(sent, sent, f_send.at[c]).wait()
    for c in range(GCH):
        sent = bs.at[c, pl.ds(0, N - 1)]
        pltpu.make_async_copy(sent, sent, b_send.at[c]).wait()
        pltpu.make_async_copy(rr1.at[c], rr1.at[c], r_send.at[c]).wait()
        pltpu.make_async_copy(cs1.at[c], cs1.at[c], c_send.at[c]).wait()
    pltpu.make_async_copy(rr2, rr2, r_send.at[GCH]).wait()
    pltpu.make_async_copy(cs2, cs2, c_send.at[GCH]).wait()
    for store in stores:
        store.wait()


def on_device(inputs, gate, cotangent, first_factor, second_factor):
    four = (B, K, C)
    any_spec = pl.BlockSpec(memory_space=pl.ANY)
    vm = pltpu.VMEM
    dma = pltpu.SemaphoreType.DMA
    mixed, gx, gf, gs = pl.pallas_call(
        kernel,
        out_shape=(
            jax.ShapeDtypeStruct(four, BF16),
            jax.ShapeDtypeStruct(four, BF16),
            jax.ShapeDtypeStruct((B, 32, K), F32),
            jax.ShapeDtypeStruct((B, 32, K), F32),
        ),
        in_specs=[any_spec] * 5,
        out_specs=(any_spec,) * 4,
        scratch_shapes=[
            vm(four, BF16), vm(four, BF16), vm(four, BF16), vm((B, K, K), BF16), vm((B, K, K), BF16),
            vm((W, B * K, 128), F32),
            vm((FCH, N, FR, C), BF16), vm((FCH, N, FR, C), BF16),
            vm((GCH, N, 16, C), BF16), vm((GCH, N, 16, C), BF16),
            vm(four, BF16), vm(four, BF16),
            vm((B, K, K), F32), vm((B, K, K), F32),
            vm((DP, B, 64, K), BF16), vm((DP - 1, B, 64, K), BF16),
            vm((GCH, DP, 2, 64, K), BF16), vm((GCH, DP - 1, 2, 64, K), BF16),
            vm((B, 32, K), BF16), vm((B, 32, K), BF16),
            vm((GCH, 2, 32, K), BF16), vm((GCH, 2, 32, K), BF16),
            vm((B, 32, K), F32), vm((B, 32, K), F32),
            dma((5, B)), dma((FCH,)), dma((FCH,)), dma((GCH,)), dma((GCH,)),
            dma((GCH + 1,)), dma((GCH + 1,)), dma((GCH + 1,)), dma((GCH + 1,)), dma((3, B)),
        ],
        compiler_params=pltpu.CompilerParams(
            collective_id=0, has_side_effects=True, vmem_limit_bytes=56 * 2**20
        ),
        cost_estimate=pl.CostEstimate(
            flops=6 * 2 * B * K * K * C, bytes_accessed=10 * 2**20, transcendentals=0
        ),
        name="monarch",
    )(
        inputs.reshape(four), gate.reshape(four), cotangent.reshape(four),
        first_factor, second_factor,
    )
    return mixed.reshape(inputs.shape), gx.reshape(inputs.shape), gf, gs


def solution(mesh):
    rows = P("dp", "seq", "chan")
    factor = P("seq", None, None)
    grad = P("seq", ("dp", "chan"), None)
    return jax.shard_map(
        on_device,
        mesh=mesh,
        in_specs=(rows, rows, rows, factor, factor),
        out_specs=(rows, rows, grad, grad),
        check_vma=False,
    )
```

time: 271 us -> 106 us (0.39)
  waiting for transfers between devices: 148 us -> 0 us
  Pallas kernels: 0 us -> 100 us
  blocking collectives: 66 us -> 0 us
  matrix products: 19 us -> 0 us
  between operations: 14.1 us -> 0.65 us
  starting transfers between devices: 10.5 us -> 0 us
  local copies, waits for them, and re-layouts: 9.6 us -> 5.39 us
  other arithmetic: 2.95 us -> 0 us
    reduce_scatter x2 -> x0, waiting for transfers between devices: 112 us -> none  [the longest x1 96.1 us: on_device(): lax.psum_scatter(grad_first_part, ('dp', 'chan'), scatter_dimension=1, ti...]
    pallas_call x0 -> x1, Pallas kernels: none -> 100 us  [on_device(): pl.pallas_call(kernel, out_shape=(jax.ShapeDtypeStruct(four, BF16), jax.S...]
    all_to_all x1 -> x0, blocking collectives: 66 us -> none  [on_device(): lax.all_to_all(grad_first_t, 'seq', split_axis=2, concat_axis=1, tiled=True)]
    all_to_all x1 -> x0, waiting for transfers between devices: 35.9 us -> none  [on_device(): lax.all_to_all(first_mixed, 'seq', split_axis=2, concat_axis=1, tiled=True)]
    dot_general x6 -> x0, matrix products: 19 us -> none  [the longest x1 5.12 us: on_device(): jnp.einsum('ikj,skic->sijc', first_factor, backward_piece, preferred_elem...]
    all_to_all x1 -> x0, starting transfers between devices: 10.4 us -> none  [on_device(): lax.all_to_all(first_mixed, 'seq', split_axis=2, concat_axis=1, tiled=True)]
    convert_element_type x2 -> x0, local copies, waits for them, and re-layouts: 4.96 us -> none  [the longest x1 2.9 us: on_device(): grad_first_t = jnp.einsum('kmi,skmc->skic', second_factor, grad_mixed, pr...]
    convert_element_type x1 -> x0, other arithmetic: 2.95 us -> none  [on_device(): grad_mixed = (cotangent.reshape(shape_four).astype(jnp.float32) * gate_bl...]
  transfers between devices with their start and end apart: 3 -> 0, of which waited for: 3 -> 0; matrix products, arithmetic and copies ran while one was open for 8% -> 0% of each run, Pallas kernels for 0% -> 0%
where the time goes in v1:
time: 106 us
  Pallas kernels  100 us (94%)
  local copies, waits for them, and re-layouts  5.39 us (5%)
    pallas_call x1, Pallas kernels, on_device(): pl.pallas_call(kernel, out_shape=(jax.ShapeDtypeStruct(four, BF16), jax.S...  100 us
    unnamed x10, local copies, waits for them, and re-layouts  5.39 us

profile of v1, /device:TPU:1, one launch (start us, length us, event | category | flops | bytes accessed | tf_op | source)
XLA Modules:
  0.0 106.0 jit_solution(2788337852667429845)
XLA Ops:
  0.6 100.0 %monarch.1 = (bf16[8,256,384]{2,1,0:T(8,128)(2,1)}, bf16[8,256,384]{2,1,0:T(8,128)(2,1)}, f32[8,32,256]{2,1,0:T(8,128)}, f32[8,32,256]{2,1,0:T(8,128)}) custom-call(bf16[8,256,384]{2,1,0:T(8,128)(2,1)} %bitcast.7, bf16[8,256,384]{2,1,0:T(8,128)(2,1)} %bitcast.8, bf16[8,256,384]{2,1,0:T(8,128)(2,1)} %bitcast.9, bf16[8,256,256]{2,1,0:T(8,128)(2,1)} %ff_h.1, ...), custom_call_target="tpu_custom_call" | custom-call | flops 2415919104 | bytes 10485760 | tf_op jit(solution)/shard_map/monarch/pallas_call | solution.py:223
  100.6 0.0 copy-start
  100.6 2.8 %copy.13 = bf16[1,2048,384]{2,1,0:T(8,128)(2,1)} copy(bf16[1,2048,384]{2,1,0:T(8,128)(2,1)} %bitcast.6) | data formatting | bytes 3145728
  103.5 0.0 copy-done
  103.5 0.0 copy-start.2
  103.5 0.0 copy-start.1
  103.5 1.1 %copy.14 = bf16[1,2048,384]{2,1,0:T(8,128)(2,1)} copy(bf16[1,2048,384]{2,1,0:T(8,128)(2,1)S(1)} %bitcast.5) | data formatting | bytes 3145728
  104.6 0.0 copy-done.2
  104.6 0.7 copy.15
  105.3 0.0 copy-done.1
  105.3 0.7 copy.16
Async XLA Ops:
  100.6 2.8 %copy-start = (bf16[8,256,384]{2,1,0:T(8,128)(2,1)S(1)}, bf16[8,256,384]{2,1,0:T(8,128)(2,1)}, u32[]{:S(2)}) copy-start(bf16[8,256,384]{2,1,0:T(8,128)(2,1)} %get-tuple-element.9) | copy-start | bytes 4718596
  103.5 1.1 %copy-start.2 = (f32[8,32,256]{2,1,0:T(8,128)S(1)}, f32[8,32,256]{2,1,0:T(8,128)}, u32[]{:S(2)}) copy-start(f32[8,32,256]{2,1,0:T(8,128)} %get-tuple-element.18) | copy-start | bytes 786436
  103.5 1.9 %copy-start.1 = (f32[8,32,256]{2,1,0:T(8,128)S(1)}, f32[8,32,256]{2,1,0:T(8,128)}, u32[]{:S(2)}) copy-start(f32[8,32,256]{2,1,0:T(8,128)} %get-tuple-element.19) | copy-start | bytes 786436

commit v2 on v1

--- a/solution.py
+++ b/solution.py
@@ -15,7 +15,7 @@
 C = 384
 W = C // 128
 DP = 4
-FCH = 2
+FCH = 4
 FR = 64 // FCH
 GCH = 4
 
@@ -26,14 +26,29 @@
 
 def kernel(
     x_h, g_h, t_h, ff_h, sf_h,
-    mixed_h, gx_h, gf_h, gs_h,
-    x_v, g_v, t_v, ff_v, sf_v, tmp, fs, fr, bs, br, mixed_v, gx_v,
-    part2, part1, rs2, rr2, rs1, rr1, cs2, cr2, cs1, cr1, out2, out1,
-    in_sem, f_send, f_recv, b_send, b_recv, r_send, r_recv, c_send, c_recv, o_sem,
+    mixed_v, gx_v, out1, out2,
+    x_v, g_v, t_v, ff_v, sf_v, tmp, fs, fr, bs, br,
+    part2, part1, rs2, rr2, rs1, rr1, cs2, cr2, cs1, cr1,
+    in_sem, f_send, f_recv, b_send, b_recv, r_send, r_recv, c_send, c_recv,
 ):
     dp = lax.axis_index("dp")
     ch = lax.axis_index("chan")
     me = lax.axis_index("seq")
+
+    barrier = pltpu.get_barrier_semaphore()
+
+    def greet(s, carry):
+        pl.semaphore_signal(
+            barrier, inc=1, device_id={"seq": lax.rem(me + s, N)}, device_id_type=MESH
+        )
+        return carry
+
+    lax.fori_loop(1, N, greet, 0)
+    for s in range(1, DP):
+        pl.semaphore_signal(
+            barrier, inc=1, device_id={"dp": lax.rem(dp + s, DP)}, device_id_type=MESH
+        )
+    pl.semaphore_signal(barrier, inc=1, device_id={"chan": 1 - ch}, device_id_type=MESH)
 
     loads = {}
     for i in range(B):
@@ -44,21 +59,6 @@
         for n, (h, v) in enumerate(((t_h, t_v), (g_h, g_v), (sf_h, sf_v))):
             loads[n + 2, i] = pltpu.make_async_copy(h.at[i], v.at[i], in_sem.at[n + 2, i])
             loads[n + 2, i].start()
-
-    barrier = pltpu.get_barrier_semaphore()
-
-    def greet(s, carry):
-        pl.semaphore_signal(
-            barrier, inc=1, device_id={"seq": lax.rem(me + s, N)}, device_id_type=MESH
-        )
-        return carry
-
-    lax.fori_loop(1, N, greet, 0)
-    for s in range(1, DP):
-        pl.semaphore_signal(
-            barrier, inc=1, device_id={"dp": lax.rem(dp + s, DP)}, device_id_type=MESH
-        )
-    pl.semaphore_signal(barrier, inc=1, device_id={"chan": 1 - ch}, device_id_type=MESH)
 
     def exchange(src, dst, c, send_sem, recv_sem):
         def one(s, carry):
@@ -156,14 +156,11 @@
             return carry
 
         lax.fori_loop(0, N, unpack, 0)
-    stores = []
     for k in range(B):
         piece = jnp.concatenate(
             [tmp[w, pl.ds(k, K, stride=B), :].astype(BF16) for w in range(W)], axis=1
         )
         mixed_v[k] = (dot(sf_v[k], piece, ((1,), (0,))) * g_v[k].astype(F32)).astype(BF16)
-        stores.append(pltpu.make_async_copy(mixed_v.at[k], mixed_h.at[k], o_sem.at[0, k]))
-        stores[-1].start()
         grad = dot(t_v[k], piece, ((1,), (1,)))
         part2[k] = grad
         for d in range(DP):
@@ -185,21 +182,15 @@
             i = 2 * c + h
             piece = chunk[:, B * h : B * h + B, :].reshape(K, C).astype(BF16)
             gx_v[i] = dot(ff_v[i], piece, ((0,), (0,))).astype(BF16)
-            stores.append(pltpu.make_async_copy(gx_v.at[i], gx_h.at[i], o_sem.at[1, i]))
-            stores[-1].start()
-        if c == 0:
+        if c == 1:
             chan_send(part2, rr2, cs2, cr2, out2, GCH, 0, B)
-        else:
+        if c > 0:
             chan_send(part1, rr1.at[c - 1], cs1.at[c - 1], cr1.at[c - 1], out1, c - 1, 2 * c - 2, 2)
     c = GCH - 1
     chan_done(cr2, out2, GCH, 0, B)
-    stores.append(pltpu.make_async_copy(out2, gs_h, o_sem.at[2, 0]))
-    stores[-1].start()
     chan_send(part1, rr1.at[c], cs1.at[c], cr1.at[c], out1, c, 2 * c, 2)
     for c in range(GCH):
         chan_done(cr1.at[c], out1, c, 2 * c, 2)
-    stores.append(pltpu.make_async_copy(out1, gf_h, o_sem.at[2, 1]))
-    stores[-1].start()
 
     for c in range(FCH):
         sent = fs.at[c, pl.ds(0, N - 1)]
@@ -211,8 +202,15 @@
         pltpu.make_async_copy(cs1.at[c], cs1.at[c], c_send.at[c]).wait()
     pltpu.make_async_copy(rr2, rr2, r_send.at[GCH]).wait()
     pltpu.make_async_copy(cs2, cs2, c_send.at[GCH]).wait()
-    for store in stores:
-        store.wait()
+
+
+def store(mixed_v, gx_v, gf_v, gs_v, mixed_h, gx_h, gf_h, gs_h, sem):
+    pairs = ((mixed_v, mixed_h), (gx_v, gx_h), (gf_v, gf_h), (gs_v, gs_h))
+    copies = [pltpu.make_async_copy(v, h, sem.at[n]) for n, (v, h) in enumerate(pairs)]
+    for copy in copies:
+        copy.start()
+    for copy in copies:
+        copy.wait()
 
 
 def on_device(inputs, gate, cotangent, first_factor, second_factor):
@@ -220,30 +218,24 @@
     any_spec = pl.BlockSpec(memory_space=pl.ANY)
     vm = pltpu.VMEM
     dma = pltpu.SemaphoreType.DMA
-    mixed, gx, gf, gs = pl.pallas_call(
+    shapes = ((four, BF16), (four, BF16), ((B, 32, K), F32), ((B, 32, K), F32))
+    results = pl.pallas_call(
         kernel,
-        out_shape=(
-            jax.ShapeDtypeStruct(four, BF16),
-            jax.ShapeDtypeStruct(four, BF16),
-            jax.ShapeDtypeStruct((B, 32, K), F32),
-            jax.ShapeDtypeStruct((B, 32, K), F32),
-        ),
+        out_shape=(vm(four, BF16), vm(four, BF16), vm((B, 32, K), F32), vm((B, 32, K), F32)),
         in_specs=[any_spec] * 5,
-        out_specs=(any_spec,) * 4,
+        out_specs=(pl.BlockSpec(memory_space=pltpu.VMEM),) * 4,
         scratch_shapes=[
             vm(four, BF16), vm(four, BF16), vm(four, BF16), vm((B, K, K), BF16), vm((B, K, K), BF16),
             vm((W, B * K, 128), F32),
             vm((FCH, N, FR, C), BF16), vm((FCH, N, FR, C), BF16),
             vm((GCH, N, 16, C), BF16), vm((GCH, N, 16, C), BF16),
-            vm(four, BF16), vm(four, BF16),
             vm((B, K, K), F32), vm((B, K, K), F32),
             vm((DP, B, 64, K), BF16), vm((DP - 1, B, 64, K), BF16),
             vm((GCH, DP, 2, 64, K), BF16), vm((GCH, DP - 1, 2, 64, K), BF16),
             vm((B, 32, K), BF16), vm((B, 32, K), BF16),
             vm((GCH, 2, 32, K), BF16), vm((GCH, 2, 32, K), BF16),
-            vm((B, 32, K), F32), vm((B, 32, K), F32),
             dma((5, B)), dma((FCH,)), dma((FCH,)), dma((GCH,)), dma((GCH,)),
-            dma((GCH + 1,)), dma((GCH + 1,)), dma((GCH + 1,)), dma((GCH + 1,)), dma((3, B)),
+            dma((GCH + 1,)), dma((GCH + 1,)), dma((GCH + 1,)), dma((GCH + 1,)),
         ],
         compiler_params=pltpu.CompilerParams(
             collective_id=0, has_side_effects=True, vmem_limit_bytes=56 * 2**20
@@ -256,6 +248,15 @@
         inputs.reshape(four), gate.reshape(four), cotangent.reshape(four),
         first_factor, second_factor,
     )
+    mixed, gx, gf, gs = pl.pallas_call(
+        store,
+        out_shape=tuple(jax.ShapeDtypeStruct(*shape) for shape in shapes),
+        in_specs=[pl.BlockSpec(memory_space=pltpu.VMEM)] * 4,
+        out_specs=(any_spec,) * 4,
+        scratch_shapes=[dma((4,))],
+        name="store",
+        compiler_params=pltpu.CompilerParams(vmem_limit_bytes=2**20),
+    )(*results)
     return mixed.reshape(inputs.shape), gx.reshape(inputs.shape), gf, gs
 
 

time: 106 us -> 96.9 us (0.914)
  local copies, waits for them, and re-layouts: 5.39 us -> 0 us
  Pallas kernels: 100 us -> 96.1 us
    unnamed x10 -> x0, local copies, waits for them, and re-layouts: 5.39 us -> none
    pallas_call x1 -> x2, Pallas kernels: 100 us -> 96.1 us  [the longest x1 94.3 us: on_device(): pl.pallas_call(kernel, out_shape=(vm(four, BF16), vm(four, BF16), vm((B,...]
where the time goes in v2:
time: 96.9 us; the launch traced here: 96.8 us
  Pallas kernels  96.1 us (99%)
    pallas_call x1, Pallas kernels, on_device(): pl.pallas_call(kernel, out_shape=(vm(four, BF16), vm(four, BF16), vm((B,...  94.3 us

profile of v2, /device:TPU:1, one launch (start us, length us, event | category | flops | bytes accessed | tf_op | source)
XLA Modules:
  0.0 96.8 jit_solution(14276374372201831025)
XLA Ops:
  0.6 94.3 %monarch.1 = (bf16[8,256,384]{2,1,0:T(8,128)(2,1)S(1)}, bf16[8,256,384]{2,1,0:T(8,128)(2,1)S(1)}, f32[8,32,256]{2,1,0:T(8,128)S(1)}, f32[8,32,256]{2,1,0:T(8,128)S(1)}) custom-call(bf16[8,256,384]{2,1,0:T(8,128)(2,1)} %bitcast.5, bf16[8,256,384]{2,1,0:T(8,128)(2,1)} %bitcast.6, bf16[8,256,384]{2,1,0:T(8,128)(2,1)} %bitcast.7, bf16[8,256,256]{2,1,0:T(8,128)(2,1)} %ff_h.1, ...), custom_call_target="tpu_custom_call" | custom-call | flops 2415919104 | bytes 10485760 | tf_op jit(solution)/shard_map/monarch/pallas_call | solution.py:222
  94.9 1.9 %store.1 = (bf16[8,256,384]{2,1,0:T(8,128)(2,1)}, bf16[8,256,384]{2,1,0:T(8,128)(2,1)}, f32[8,32,256]{2,1,0:T(8,128)}, f32[8,32,256]{2,1,0:T(8,128)}) custom-call(bf16[8,256,384]{2,1,0:T(8,128)(2,1)S(1)} %get-tuple-element.12.mixed_v, bf16[8,256,384]{2,1,0:T(8,128)(2,1)S(1)} %get-tuple-element.13.gx_v, f32[8,32,256]{2,1,0:T(8,128)S(1)} %get-tuple-element.14.gf_v, ...), custom_call_target="tpu_custom_call" | custom-call | tf_op jit(solution)/shard_map/store/pallas_call | solution.py:251

commit v3 on v2

--- a/solution.py
+++ b/solution.py
@@ -178,17 +178,19 @@
             for d in range(DP):
                 rs1[c, d, h] = grad[64 * d : 64 * d + 64].astype(BF16)
         reduce_send(rs1.at[c], rr1.at[c], c)
+        if c == 2:
+            chan_send(part2, rr2, cs2, cr2, out2, GCH, 0, B)
+        for p in {2: (0, 1), 3: (2,)}.get(c, ()):
+            chan_send(part1, rr1.at[p], cs1.at[p], cr1.at[p], out1, p, 2 * p, 2)
+    for c in range(GCH):
+        chunk = br[c].astype(F32)
         for h in range(2):
             i = 2 * c + h
             piece = chunk[:, B * h : B * h + B, :].reshape(K, C).astype(BF16)
             gx_v[i] = dot(ff_v[i], piece, ((0,), (0,))).astype(BF16)
-        if c == 1:
-            chan_send(part2, rr2, cs2, cr2, out2, GCH, 0, B)
-        if c > 0:
-            chan_send(part1, rr1.at[c - 1], cs1.at[c - 1], cr1.at[c - 1], out1, c - 1, 2 * c - 2, 2)
     c = GCH - 1
+    chan_send(part1, rr1.at[c], cs1.at[c], cr1.at[c], out1, c, 2 * c, 2)
     chan_done(cr2, out2, GCH, 0, B)
-    chan_send(part1, rr1.at[c], cs1.at[c], cr1.at[c], out1, c, 2 * c, 2)
     for c in range(GCH):
         chan_done(cr1.at[c], out1, c, 2 * c, 2)
 

time: 96.9 us -> 96.9 us (level)
  no operation moved by 1% of the time
where the time goes in v3:
time: 96.9 us; the launch traced here: 96.8 us
  Pallas kernels  96.1 us (99%)
    pallas_call x1, Pallas kernels, on_device(): pl.pallas_call(kernel, out_shape=(vm(four, BF16), vm(four, BF16), vm((B,...  94.3 us

profile of v3, /device:TPU:1, one launch (start us, length us, event | category | flops | bytes accessed | tf_op | source)
XLA Modules:
  0.0 96.8 jit_solution(16862907121003282931)
XLA Ops:
  0.6 94.3 %monarch.1 = (bf16[8,256,384]{2,1,0:T(8,128)(2,1)S(1)}, bf16[8,256,384]{2,1,0:T(8,128)(2,1)S(1)}, f32[8,32,256]{2,1,0:T(8,128)S(1)}, f32[8,32,256]{2,1,0:T(8,128)S(1)}) custom-call(bf16[8,256,384]{2,1,0:T(8,128)(2,1)} %bitcast.5, bf16[8,256,384]{2,1,0:T(8,128)(2,1)} %bitcast.6, bf16[8,256,384]{2,1,0:T(8,128)(2,1)} %bitcast.7, bf16[8,256,256]{2,1,0:T(8,128)(2,1)} %ff_h.1, ...), custom_call_target="tpu_custom_call" | custom-call | flops 2415919104 | bytes 10485760 | tf_op jit(solution)/shard_map/monarch/pallas_call | solution.py:224
  94.9 1.9 %store.1 = (bf16[8,256,384]{2,1,0:T(8,128)(2,1)}, bf16[8,256,384]{2,1,0:T(8,128)(2,1)}, f32[8,32,256]{2,1,0:T(8,128)}, f32[8,32,256]{2,1,0:T(8,128)}) custom-call(bf16[8,256,384]{2,1,0:T(8,128)(2,1)S(1)} %get-tuple-element.12.mixed_v, bf16[8,256,384]{2,1,0:T(8,128)(2,1)S(1)} %get-tuple-element.13.gx_v, f32[8,32,256]{2,1,0:T(8,128)S(1)} %get-tuple-element.14.gf_v, ...), custom_call_target="tpu_custom_call" | custom-call | tf_op jit(solution)/shard_map/store/pallas_call | solution.py:253
